TPU v7x, 512 devices: a whole 4x8x8 slice. The times are simulated.
512 devices in a mesh: ep: 128 (over z, y, core), dp: 4 (over x).
Axes of the slice: x: 4, y: 8, z: 8, core: 2. Of those that a mesh axis runs over, the one named last changes fastest.
Arguments:
- tokens: bfloat16 [65536, 2048], P(('dp', 'ep')), parts along dimension 0, may hold values from -6 to 6
- expert_ids: int32 [65536, 4], P(('dp', 'ep')), parts along dimension 0, may hold values from 0 to 127, all different within a row; in each aligned block of 128 rows (0 to 127, 128 to 255, ...) at most 6 rows name the same one
- gate_values: float32 [65536, 4], P(('dp', 'ep')), parts along dimension 0, may hold values from 0.1 to 1
- latent_down: bfloat16 [2048, 512], P('ep'), may hold values from -0.125 to 0.125
- latent_up: bfloat16 [512, 2048], P(None, 'ep'), may hold values from -0.25 to 0.25
- expert_up: bfloat16 [128, 512, 1408], P('ep'), may hold values from -0.25 to 0.25
- expert_down: bfloat16 [128, 1408, 512], P('ep'), may hold values from -0.15625 to 0.15625
- grad_out: bfloat16 [65536, 2048], P(('dp', 'ep')), parts along dimension 0, may hold values from -6 to 6
Outputs:
- layer_out: bfloat16 [65536, 2048], P(('dp', 'ep')), parts along dimension 0
- grad_tokens: bfloat16 [65536, 2048], P(('dp', 'ep')), parts along dimension 0
There are 4 independent parts, one for each index of `dp`. A program takes and returns all parts, laid end to end along the dimension named above; an argument that names none is the same for every part. Nothing has to cross between parts.
Inputs may be any that keep to these rules, and one draw needn't show every extreme that they name: `expert_ids`: each row names 4 different experts. Among the 128 tokens of one device, no expert is named by more than 6 tokens, and in every draw some expert is named by exactly 6 tokens of some device.
All inputs are finite; a program needn't handle non-finite values.
Results may differ from a plain program's by a relative error of at most 0.013.
Values may be sent and summed in bfloat16 or wider, within the bound.
No kernel may reach another device: no remote copies, remote signals or barrier semaphores. Data moves between devices by JAX's collectives and lax.ppermute only.
A program may use at most 64 MiB of HBM per device.

v0:
```python
import jax
import jax.numpy as jnp
from jax import lax
from jax.sharding import PartitionSpec as P


def contract_last(left, right):
    return lax.dot_general(
        left, right, (((1,), (1,)), ((), ())), preferred_element_type=jnp.float32
    )


def on_device(
    tokens, expert_ids, gate_values, latent_down, latent_up, expert_up, expert_down, grad_out
):
    ep_size = lax.axis_size("ep")
    tok_rows = expert_ids.shape[0]
    top_count = expert_ids.shape[1]
    local_experts = expert_up.shape[0]
    width = latent_up.shape[0]
    experts = local_experts * ep_size
    capacity = max(2, (3 * tok_rows * top_count + 2 * experts - 1) // (2 * experts))
    full_down, full_up = (
        lax.all_gather(latent_down, "ep", axis=0, tiled=True),
        lax.all_gather(latent_up, "ep", axis=1, tiled=True),
    )
    latent = jnp.dot(tokens, full_down, preferred_element_type=jnp.float32).astype(jnp.bfloat16)
    numbers = jnp.arange(experts, dtype=jnp.int32)
    picked = (expert_ids[:, :, None] == numbers[None, None, :]).astype(jnp.int32)
    routed = jnp.sum(picked, axis=1)
    before = jnp.cumsum(routed, axis=0) - routed
    slot_pos = jnp.sum(picked * before[:, None, :], axis=2)
    flat_slot = expert_ids * capacity + slot_pos
    positions = jnp.arange(experts * capacity, dtype=jnp.int32)
    matches = flat_slot[None, :, :] == positions[:, None, None]
    placing = jnp.any(matches, axis=2).astype(jnp.bfloat16)
    gate_place = jnp.sum(jnp.where(matches, gate_values[None, :, :], 0.0), axis=2)
    outbound = jnp.dot(placing, latent, preferred_element_type=jnp.float32).astype(jnp.bfloat16)
    outbound = outbound.reshape(ep_size, local_experts, capacity, width)
    pre_act = jnp.einsum(
        "sjml,jlf->sjmf",
        lax.all_to_all(outbound, "ep", split_axis=0, concat_axis=0, tiled=True),
        expert_up,
        preferred_element_type=jnp.float32,
    )
    squared = jnp.square(jax.nn.relu(pre_act)).astype(jnp.bfloat16)
    expert_out = jnp.einsum(
        "sjmf,jfl->sjml", squared, expert_down, preferred_element_type=jnp.float32
    ).astype(jnp.bfloat16)
    expert_out, stored = (expert_out, pre_act)
    returned = lax.all_to_all(expert_out, "ep", split_axis=0, concat_axis=0, tiled=True).reshape(
        experts * capacity, width
    )
    gathered_rows = jnp.take(returned, flat_slot, axis=0)
    combined = jnp.sum(gate_values[:, :, None] * gathered_rows.astype(jnp.float32), axis=1).astype(
        jnp.bfloat16
    )
    layer_full = jnp.dot(combined, full_up, preferred_element_type=jnp.float32)
    grad_latent = contract_last(grad_out, full_up)
    layer_out = layer_full.astype(jnp.bfloat16)
    grad_send = jnp.dot(
        gate_place, grad_latent, precision=lax.Precision.HIGHEST, preferred_element_type=jnp.float32
    )
    grad_send = grad_send.astype(jnp.bfloat16).reshape(ep_size, local_experts, capacity, width)
    grad_arrived = lax.all_to_all(grad_send, "ep", split_axis=0, concat_axis=0, tiled=True)
    pre_act = stored
    grad_act = jnp.einsum(
        "sjml,jfl->sjmf", grad_arrived, expert_down, preferred_element_type=jnp.float32
    )
    grad_pre = (2.0 * jax.nn.relu(pre_act) * grad_act).astype(jnp.bfloat16)
    grad_in = jnp.einsum(
        "sjmf,jlf->sjml", grad_pre, expert_up, preferred_element_type=jnp.float32
    ).astype(jnp.bfloat16)
    grad_back = lax.all_to_all(grad_in, "ep", split_axis=0, concat_axis=0, tiled=True).reshape(
        experts * capacity, width
    )
    grad_sum = jnp.sum(jnp.take(grad_back, flat_slot, axis=0).astype(jnp.float32), axis=1).astype(
        jnp.bfloat16
    )
    grad_tokens = contract_last(grad_sum, full_down).astype(jnp.bfloat16)
    return (layer_out, grad_tokens)


def solution(mesh):
    placed = (
        P(("dp", "ep"), None),
        P(("dp", "ep"), None),
        P(("dp", "ep"), None),
        P("ep", None),
        P(None, "ep"),
        P("ep", None, None),
        P("ep", None, None),
        P(("dp", "ep"), None),
    )
    return jax.shard_map(
        on_device,
        mesh=mesh,
        in_specs=placed,
        out_specs=(P(("dp", "ep"), None), P(("dp", "ep"), None)),
        check_vma=False,
    )
```

profile of v0, /device:TPU:1, one launch (start us, length us, event | category | flops | bytes accessed | tf_op | source)
XLA Modules:
  0.0 342.6 jit_solution(10094555136022475105)
XLA Ops:
  12.0 87.9 %all-gather.3.cloned.1.call-done = bf16[2048,512]{1,0:T(8,128)(2,1)} async-done(((bf16[16,512]{1,0:T(8,128)(2,1)}), bf16[2048,512]{1,0:T(8,128)(2,1)}) %all-gather.3.cloned.1.call-update) | async-done | bytes 2097168 | tf_op jit(solution)/shard_map/all_gather | solution.py:24
  99.9 2.6 convolution_convert_fusion.3
  103.8 9.5 %all-to-all-start = ((bf16[128,1,6,512]{3,2,1,0:T(8,128)(2,1)}), bf16[128,1,6,512]{3,2,1,0:T(8,128)(2,1)S(1)}, u32[]{:S(2)}, u32[]{:S(2)}) async-start(bf16[128,1,6,512]{3,2,1,0:T(8,128)(2,1)} %bitcast), calls=%async_computation | async-start | bytes 2097152 | tf_op jit(solution)/shard_map/all_to_all | solution.py:42
  114.2 81.3 %all-gather.5.cloned.1.call-done = bf16[512,2048]{0,1:T(8,128)(2,1)} async-done(((bf16[512,16]{0,1:T(8,128)(2,1)}), bf16[512,2048]{0,1:T(8,128)(2,1)}) %all-gather.5.cloned.1.call-update) | async-done | bytes 2097168 | tf_op jit(solution)/shard_map/all_gather | solution.py:25
  195.5 2.1 fusion.33
  197.6 1.4 convolution_convert_fusion.2
  200.3 9.5 %all-to-all-start.2 = ((bf16[128,1,6,512]{3,2,1,0:T(8,128)(2,1)}), bf16[128,1,6,512]{3,2,1,0:T(8,128)(2,1)S(1)}, u32[]{:S(2)}, u32[]{:S(2)}) async-start(bf16[128,1,6,512]{3,2,1,0:T(8,128)(2,1)} %bitcast.9), calls=%async_computation.2 | async-start | bytes 2097152 | tf_op jit(solution)/shard_map/all_to_all | solution.py:65
  209.9 3.4 fusion.7
  213.3 27.5 %all-to-all-done.2 = bf16[128,1,6,512]{3,2,1,0:T(8,128)(2,1)S(1)} async-done(((bf16[128,1,6,512]{3,2,1,0:T(8,128)(2,1)}), bf16[128,1,6,512]{3,2,1,0:T(8,128)(2,1)S(1)}, u32[]{:S(2)}, u32[]{:S(2)}) %all-to-all-start.2) | async-done | bytes 786464 | tf_op jit(solution)/shard_map/all_to_all | solution.py:65
  240.8 5.4 %fusion.18 = bf16[128,1,6,512]{3,0,2,1:T(8,128)(2,1)S(1)} fusion(bf16[1,512,1408]{2,1,0:T(8,128)(2,1)S(1)} %copy-done, f32[128,6,1408]{2,0,1:T(8,128)} %fusion.7, bf16[1,1408,512]{2,1,0:T(8,128)(2,1)} %param.16, bf16[128,1,6,512]{3,2,1,0:T(8,128)(2,1)S(1)} %all-to-all-done.2), kind=kOutput, calls=%fused_computation.22 | convolution fusion | flops 2219311104 | bytes 8781824 | tf_op jit(solution)/shard_map/sjmf,jlf->sjml/dot_general | solution.py:71
  246.2 1.5 copy.51
  247.7 6.5 %all-to-all-start.3 = ((bf16[128,1,6,512]{3,2,1,0:T(8,128)(2,1)}), bf16[128,1,6,512]{3,2,1,0:T(8,128)(2,1)S(1)}, u32[]{:S(2)}, u32[]{:S(2)}) async-start(bf16[128,1,6,512]{3,2,1,0:T(8,128)(2,1)} %copy.51), calls=%async_computation.3 | async-start | bytes 2097152 | tf_op jit(solution)/shard_map/all_to_all | solution.py:74
  254.2 4.0 %fusion.15 = bf16[128,1,6,512]{3,0,2,1:T(8,128)(2,1)S(1)} fusion(bf16[1,1408,512]{2,1,0:T(8,128)(2,1)} %param.16, f32[128,6,1408]{2,0,1:T(8,128)} %fusion.7), kind=kOutput, calls=%fused_computation.21 | convolution fusion | flops 1110933504 | bytes 6553600 | tf_op jit(solution)/shard_map/sjmf,jfl->sjml/dot_general | solution.py:47
  258.3 1.4 copy.46
  259.7 25.4 %all-to-all-done.3 = bf16[128,1,6,512]{3,2,1,0:T(8,128)(2,1)S(1)} async-done(((bf16[128,1,6,512]{3,2,1,0:T(8,128)(2,1)}), bf16[128,1,6,512]{3,2,1,0:T(8,128)(2,1)S(1)}, u32[]{:S(2)}, u32[]{:S(2)}) %all-to-all-start.3) | async-done | bytes 786464 | tf_op jit(solution)/shard_map/all_to_all | solution.py:74
  285.1 6.9 %all-to-all-start.1 = ((bf16[128,1,6,512]{3,2,1,0:T(8,128)(2,1)}), bf16[128,1,6,512]{3,2,1,0:T(8,128)(2,1)}, u32[]{:S(2)}, u32[]{:S(2)}) async-start(bf16[128,1,6,512]{3,2,1,0:T(8,128)(2,1)} %copy.46), calls=%async_computation.1 | async-start | bytes 2097152 | tf_op jit(solution)/shard_map/all_to_all | solution.py:51
  293.4 2.0 gather_fusion.1
  296.3 26.3 %all-to-all-done.1 = bf16[128,1,6,512]{3,2,1,0:T(8,128)(2,1)} async-done(((bf16[128,1,6,512]{3,2,1,0:T(8,128)(2,1)}), bf16[128,1,6,512]{3,2,1,0:T(8,128)(2,1)}, u32[]{:S(2)}, u32[]{:S(2)}) %all-to-all-start.1) | async-done | bytes 786464 | tf_op jit(solution)/shard_map/all_to_all | solution.py:51
  324.0 2.6 gather_fusion
  326.6 2.1 reshape.98
  328.7 1.8 select_reduce_fusion.1
  330.6 1.9 multiply_reduce_fusion
  332.5 1.6 convolution_convert_fusion
  334.1 1.6 convolution_convert_fusion.1
  (37 shorter events, 12.0 us)
Async XLA Ops:
  7.2 202.7 %copy-start = (bf16[1,512,1408]{2,1,0:T(8,128)(2,1)S(1)}, bf16[1,512,1408]{2,1,0:T(8,128)(2,1)}, u32[]{:S(2)}) copy-start(bf16[1,512,1408]{2,1,0:T(8,128)(2,1)} %param.15) | copy-start | bytes 4325380
  7.2 92.8 %all-gather.3.cloned.1.call-start = ((), (), s32[]{:S(2)}) async-start(), calls=%async_computation.4 | async-start | bytes 2113536 | tf_op jit(solution)/shard_map/all_gather | solution.py:24
  7.9 187.6 %all-gather.5.cloned.1.call-start = ((), (), s32[]{:S(2)}) async-start(), calls=%async_computation.5 | async-start | bytes 2113536 | tf_op jit(solution)/shard_map/all_gather | solution.py:25
  102.5 10.8 %copy-start.5 = (f32[128,4]{0,1:T(4,128)S(1)}, f32[128,4]{0,1:T(4,128)}, u32[]{:S(2)}) copy-start(f32[128,4]{0,1:T(4,128)} %param.12) | copy-start | bytes 6148
  102.5 93.0 %copy-start.4 = (bf16[128,2048]{1,0:T(8,128)(2,1)S(1)}, bf16[128,2048]{1,0:T(8,128)(2,1)}, u32[]{:S(2)}) copy-start(bf16[128,2048]{1,0:T(8,128)(2,1)} %param.17) | copy-start | bytes 1572868
  103.8 96.6 %all-to-all-start = ((bf16[128,1,6,512]{3,2,1,0:T(8,128)(2,1)}), bf16[128,1,6,512]{3,2,1,0:T(8,128)(2,1)S(1)}, u32[]{:S(2)}, u32[]{:S(2)}) async-start(bf16[128,1,6,512]{3,2,1,0:T(8,128)(2,1)} %bitcast), calls=%async_computation | async-start | bytes 2097152 | tf_op jit(solution)/shard_map/all_to_all | solution.py:42
  195.5 2.1 copy-start.3
  200.3 40.4 %all-to-all-start.2 = ((bf16[128,1,6,512]{3,2,1,0:T(8,128)(2,1)}), bf16[128,1,6,512]{3,2,1,0:T(8,128)(2,1)S(1)}, u32[]{:S(2)}, u32[]{:S(2)}) async-start(bf16[128,1,6,512]{3,2,1,0:T(8,128)(2,1)} %bitcast.9), calls=%async_computation.2 | async-start | bytes 2097152 | tf_op jit(solution)/shard_map/all_to_all | solution.py:65
  247.7 37.4 %all-to-all-start.3 = ((bf16[128,1,6,512]{3,2,1,0:T(8,128)(2,1)}), bf16[128,1,6,512]{3,2,1,0:T(8,128)(2,1)S(1)}, u32[]{:S(2)}, u32[]{:S(2)}) async-start(bf16[128,1,6,512]{3,2,1,0:T(8,128)(2,1)} %copy.51), calls=%async_computation.3 | async-start | bytes 2097152 | tf_op jit(solution)/shard_map/all_to_all | solution.py:74
  258.2 34.7 %copy-start.6 = (pred[128,4]{0,1:T(4,128)(4,1)S(1)}, pred[128,4]{0,1:T(4,128)(4,1)}, u32[]{:S(2)}) copy-start(pred[128,4]{0,1:T(4,128)(4,1)} %get-tuple-element.3) | copy-start | bytes 1540
  285.1 37.5 %all-to-all-start.1 = ((bf16[128,1,6,512]{3,2,1,0:T(8,128)(2,1)}), bf16[128,1,6,512]{3,2,1,0:T(8,128)(2,1)}, u32[]{:S(2)}, u32[]{:S(2)}) async-start(bf16[128,1,6,512]{3,2,1,0:T(8,128)(2,1)} %copy.46), calls=%async_computation.1 | async-start | bytes 2097152 | tf_op jit(solution)/shard_map/all_to_all | solution.py:51
  326.6 5.9 %copy-start.1 = (bf16[2048,512]{1,0:T(8,128)(2,1)S(1)}, bf16[2048,512]{1,0:T(8,128)(2,1)}, u32[]{:S(2)}) copy-start(bf16[2048,512]{1,0:T(8,128)(2,1)} %all-gather.3.cloned.1.call-done) | copy-start | bytes 6291460
  328.7 5.4 %copy-start.2 = (bf16[512,2048]{0,1:T(8,128)(2,1)S(1)}, bf16[512,2048]{0,1:T(8,128)(2,1)}, u32[]{:S(2)}) copy-start(bf16[512,2048]{0,1:T(8,128)(2,1)} %all-gather.5.cloned.1.call-done) | copy-start | bytes 6291460
Sparse Core Ops, SparseCore 0:
  11.1 88.7 all-gather.2
  103.1 92.4 all-gather.4
where the time goes:
time: 343 us
  waiting for transfers between devices  250 us (73%)
  starting transfers between devices  32.5 us (9%)
  matrix products  22.1 us (6%)
  local copies, waits for them, and re-layouts  15.9 us (5%)
  between operations  14.2 us (4%)
  other arithmetic  8.04 us (2%)
    all_gather x1, waiting for transfers between devices, on_device(): lax.all_gather(latent_down, 'ep', axis=0, tiled=True)  87.9 us
    all_gather x1, waiting for transfers between devices, on_device(): lax.all_gather(latent_up, 'ep', axis=1, tiled=True)  81.3 us
    all_to_all x1, waiting for transfers between devices, on_device(): lax.all_to_all(grad_send, 'ep', split_axis=0, concat_axis=0, tiled=True)  27.5 us
    all_to_all x1, waiting for transfers between devices, on_device(): lax.all_to_all(expert_out, 'ep', split_axis=0, concat_axis=0, tiled=True)  26.3 us
    all_to_all x1, waiting for transfers between devices, on_device(): lax.all_to_all(grad_in, 'ep', split_axis=0, concat_axis=0, tiled=True)  25.4 us
    all_to_all x1, starting transfers between devices, on_device(): lax.all_to_all(outbound, 'ep', split_axis=0, concat_axis=0, tiled=True)  9.51 us
    all_to_all x1, starting transfers between devices, on_device(): lax.all_to_all(grad_send, 'ep', split_axis=0, concat_axis=0, tiled=True)  9.5 us
    all_to_all x1, starting transfers between devices, on_device(): lax.all_to_all(expert_out, 'ep', split_axis=0, concat_axis=0, tiled=True)  6.94 us
  transfers between devices with their start and end apart: 6, of which 5 were waited for; matrix products, arithmetic and copies ran while one was open for 8% of the time, Pallas kernels for 0%

commit v1 on v0

--- a/solution.py
+++ b/solution.py
@@ -2,6 +2,13 @@
 import jax.numpy as jnp
 from jax import lax
 from jax.sharding import PartitionSpec as P
+
+
+def all_by_exchange(x, axis, dim):
+    count = lax.axis_size(axis)
+    parts = jnp.stack([x for _ in range(count)])
+    parts = lax.all_to_all(parts, axis, split_axis=0, concat_axis=0)
+    return jnp.concatenate(parts, axis=dim)
 
 
 def contract_last(left, right):
@@ -21,7 +28,7 @@
     experts = local_experts * ep_size
     capacity = max(2, (3 * tok_rows * top_count + 2 * experts - 1) // (2 * experts))
     full_down, full_up = (
-        lax.all_gather(latent_down, "ep", axis=0, tiled=True),
+        all_by_exchange(latent_down, "ep", 0),
         lax.all_gather(latent_up, "ep", axis=1, tiled=True),
     )
     latent = jnp.dot(tokens, full_down, preferred_element_type=jnp.float32).astype(jnp.bfloat16)

time: 343 us -> 286 us (0.83)
  waiting for transfers between devices: 250 us -> 169 us
  starting transfers between devices: 32.5 us -> 51.2 us
  matrix products: 22.1 us -> 26 us
    all_gather x1 -> x0, waiting for transfers between devices: 87.9 us -> none  [on_device(): lax.all_gather(latent_down, 'ep', axis=0, tiled=True)]
    all_to_all x0 -> x1, waiting for transfers between devices: none -> 46.3 us  [all_by_exchange(): parts = lax.all_to_all(parts, axis, split_axis=0, concat_axis=0)]
    all_gather x1, waiting for transfers between devices: 81.3 us -> 47.7 us  [on_device(): lax.all_gather(latent_up, 'ep', axis=1, tiled=True)]
    all_to_all x0 -> x1, starting transfers between devices: none -> 18.6 us  [all_by_exchange(): parts = lax.all_to_all(parts, axis, split_axis=0, concat_axis=0)]
    all_to_all x1, waiting for transfers between devices: 26.3 us -> 21.4 us  [on_device(): lax.all_to_all(expert_out, 'ep', split_axis=0, concat_axis=0, tiled=True)]
  transfers between devices with their start and end apart: 6 -> 6, of which waited for: 5 -> 5; matrix products, arithmetic and copies ran while one was open for 8% -> 12% of each run, Pallas kernels for 0% -> 0%
where the time goes in v1:
time: 286 us; the launch traced here: 285 us
  waiting for transfers between devices  169 us (59%)
  starting transfers between devices  51.2 us (18%)
  matrix products  26 us (9%)
  local copies, waits for them, and re-layouts  17.9 us (6%)
  between operations  14.2 us (5%)
  other arithmetic  6.81 us (2%)
    all_gather x1, waiting for transfers between devices, on_device(): lax.all_gather(latent_up, 'ep', axis=1, tiled=True)  47.7 us
    all_to_all x1, waiting for transfers between devices, all_by_exchange(): parts = lax.all_to_all(parts, axis, split_axis=0, concat_axis=0)  46.3 us
    all_to_all x1, waiting for transfers between devices, on_device(): lax.all_to_all(grad_send, 'ep', split_axis=0, concat_axis=0, tiled=True)  27.5 us
    all_to_all x1, waiting for transfers between devices, on_device(): lax.all_to_all(grad_in, 'ep', split_axis=0, concat_axis=0, tiled=True)  25.4 us
    all_to_all x1, waiting for transfers between devices, on_device(): lax.all_to_all(expert_out, 'ep', split_axis=0, concat_axis=0, tiled=True)  21.4 us
    all_to_all x1, starting transfers between devices, all_by_exchange(): parts = lax.all_to_all(parts, axis, split_axis=0, concat_axis=0)  18.6 us
    all_to_all x1, starting transfers between devices, on_device(): lax.all_to_all(grad_send, 'ep', split_axis=0, concat_axis=0, tiled=True)  10.6 us
    all_to_all x1, starting transfers between devices, on_device(): lax.all_to_all(outbound, 'ep', split_axis=0, concat_axis=0, tiled=True)  9.07 us
  transfers between devices with their start and end apart: 6, of which 5 were waited for; matrix products, arithmetic and copies ran while one was open for 12% of the time, Pallas kernels for 0%

profile of v1, /device:TPU:1, one launch (start us, length us, event | category | flops | bytes accessed | tf_op | source)
XLA Modules:
  0.0 285.2 jit_solution(16598632800757022513)
XLA Ops:
  7.2 2.4 stack.2
  9.6 18.6 %all-to-all-start = ((bf16[128,16,512]{2,1,0:T(8,128)(2,1)}), bf16[128,16,512]{2,1,0:T(8,128)(2,1)S(1)}, u32[]{:S(2)}, u32[]{:S(2)}) async-start(bf16[128,16,512]{2,1,0:T(8,128)(2,1)} %stack.2), calls=%async_computation | async-start | bytes 4194304 | tf_op jit(solution)/shard_map/all_to_all | solution.py:10
  29.7 1.6 reduce_window_sum.11
  33.3 46.3 %all-to-all-done = bf16[128,16,512]{2,1,0:T(8,128)(2,1)S(1)} async-done(((bf16[128,16,512]{2,1,0:T(8,128)(2,1)}), bf16[128,16,512]{2,1,0:T(8,128)(2,1)S(1)}, u32[]{:S(2)}, u32[]{:S(2)}) %all-to-all-start) | async-done | bytes 2097184 | tf_op jit(solution)/shard_map/all_to_all | solution.py:10
  79.7 3.3 %convolution_convert_fusion.3 = bf16[768,512]{1,0:T(8,128)(2,1)} fusion(pred[768,128]{1,0:T(8,128)(4,1)} %fusion.2, bf16[128,2048]{1,0:T(8,128)(2,1)} %param.10, bf16[2048,512]{1,0:T(8,128)(2,1)S(1)} %bitcast.55), kind=kOutput, calls=%fused_computation.20 | convolution fusion | flops 369557504 | bytes 3506176 | tf_op jit(solution)/shard_map/dot_general | solution.py:45
  82.9 2.2 reshape.72
  85.1 9.1 %all-to-all-start.1 = ((bf16[128,1,6,512]{3,2,1,0:T(8,128)(2,1)}), bf16[128,1,6,512]{3,2,1,0:T(8,128)(2,1)S(1)}, u32[]{:S(2)}, u32[]{:S(2)}) async-start(bf16[128,1,6,512]{3,2,1,0:T(8,128)(2,1)} %bitcast.57), calls=%async_computation.1 | async-start | bytes 2097152 | tf_op jit(solution)/shard_map/all_to_all | solution.py:49
  95.1 47.7 %all-gather.2.cloned.1.call-done = bf16[512,2048]{0,1:T(8,128)(2,1)} async-done(((bf16[512,16]{0,1:T(8,128)(2,1)}), bf16[512,2048]{0,1:T(8,128)(2,1)}) %all-gather.2.cloned.1.call-update) | async-done | bytes 2097168 | tf_op jit(solution)/shard_map/all_gather | solution.py:32
  142.8 2.1 fusion.33
  147.6 10.6 %all-to-all-start.3 = ((bf16[128,1,6,512]{3,2,1,0:T(8,128)(2,1)}), bf16[128,1,6,512]{3,2,1,0:T(8,128)(2,1)S(1)}, u32[]{:S(2)}, u32[]{:S(2)}) async-start(bf16[128,1,6,512]{3,2,1,0:T(8,128)(2,1)} %bitcast.10), calls=%async_computation.3 | async-start | bytes 2097152 | tf_op jit(solution)/shard_map/all_to_all | solution.py:72
  158.3 3.4 %fusion.7 = f32[128,6,1408]{2,0,1:T(8,128)} fusion(bf16[1,512,1408]{2,1,0:T(8,128)(2,1)S(1)} %copy-done, bf16[128,1,6,512]{3,2,1,0:T(8,128)(2,1)S(1)} %all-to-all-done.1), kind=kOutput, calls=%fused_computation.15 | convolution fusion | flops 1107296256 | bytes 6553600 | tf_op jit(solution)/shard_map/sjml,jlf->sjmf/dot_general | solution.py:47
  161.7 27.5 %all-to-all-done.3 = bf16[128,1,6,512]{3,2,1,0:T(8,128)(2,1)S(1)} async-done(((bf16[128,1,6,512]{3,2,1,0:T(8,128)(2,1)}), bf16[128,1,6,512]{3,2,1,0:T(8,128)(2,1)S(1)}, u32[]{:S(2)}, u32[]{:S(2)}) %all-to-all-start.3) | async-done | bytes 786464 | tf_op jit(solution)/shard_map/all_to_all | solution.py:72
  189.2 5.4 %fusion.18 = bf16[128,1,6,512]{3,0,2,1:T(8,128)(2,1)S(1)} fusion(bf16[1,512,1408]{2,1,0:T(8,128)(2,1)S(1)} %copy-done, f32[128,6,1408]{2,0,1:T(8,128)} %fusion.7, bf16[1,1408,512]{2,1,0:T(8,128)(2,1)} %param.16, bf16[128,1,6,512]{3,2,1,0:T(8,128)(2,1)S(1)} %all-to-all-done.3), kind=kOutput, calls=%fused_computation.22 | convolution fusion | flops 2219311104 | bytes 8781824 | tf_op jit(solution)/shard_map/sjmf,jlf->sjml/dot_general | solution.py:78
  194.6 1.5 copy.51
  196.1 6.5 %all-to-all-start.4 = ((bf16[128,1,6,512]{3,2,1,0:T(8,128)(2,1)}), bf16[128,1,6,512]{3,2,1,0:T(8,128)(2,1)S(1)}, u32[]{:S(2)}, u32[]{:S(2)}) async-start(bf16[128,1,6,512]{3,2,1,0:T(8,128)(2,1)} %copy.51), calls=%async_computation.4 | async-start | bytes 2097152 | tf_op jit(solution)/shard_map/all_to_all | solution.py:81
  202.6 4.1 %fusion.15 = bf16[128,1,6,512]{3,0,2,1:T(8,128)(2,1)S(1)} fusion(bf16[1,1408,512]{2,1,0:T(8,128)(2,1)} %param.16, f32[128,6,1408]{2,0,1:T(8,128)} %fusion.7), kind=kOutput, calls=%fused_computation.21 | convolution fusion | flops 1110933504 | bytes 6553600 | tf_op jit(solution)/shard_map/sjmf,jfl->sjml/dot_general | solution.py:54
  206.7 1.4 copy.46
  208.1 25.4 %all-to-all-done.4 = bf16[128,1,6,512]{3,2,1,0:T(8,128)(2,1)S(1)} async-done(((bf16[128,1,6,512]{3,2,1,0:T(8,128)(2,1)}), bf16[128,1,6,512]{3,2,1,0:T(8,128)(2,1)S(1)}, u32[]{:S(2)}, u32[]{:S(2)}) %all-to-all-start.4) | async-done | bytes 786464 | tf_op jit(solution)/shard_map/all_to_all | solution.py:81
  234.5 6.5 %all-to-all-start.2 = ((bf16[128,1,6,512]{3,2,1,0:T(8,128)(2,1)}), bf16[128,1,6,512]{3,2,1,0:T(8,128)(2,1)S(1)}, u32[]{:S(2)}, u32[]{:S(2)}) async-start(bf16[128,1,6,512]{3,2,1,0:T(8,128)(2,1)} %copy.46), calls=%async_computation.2 | async-start | bytes 2097152 | tf_op jit(solution)/shard_map/all_to_all | solution.py:58
  242.9 2.6 gather_fusion.1
  247.4 3.2 %convolution_convert_fusion = bf16[128,2048]{1,0:T(8,128)(2,1)} fusion(bf16[128,512]{1,0:T(8,128)(2,1)S(1)} %select_reduce_fusion.1, bf16[2048,512]{1,0:T(8,128)(2,1)} %bitcast.56), kind=kOutput, calls=%fused_computation.4 | convolution fusion | flops 268697600 | bytes 2752512 | tf_op jit(solution)/shard_map/dot_general | solution.py:15
  250.6 21.4 %all-to-all-done.2 = bf16[128,1,6,512]{3,2,1,0:T(8,128)(2,1)S(1)} async-done(((bf16[128,1,6,512]{3,2,1,0:T(8,128)(2,1)}), bf16[128,1,6,512]{3,2,1,0:T(8,128)(2,1)S(1)}, u32[]{:S(2)}, u32[]{:S(2)}) %all-to-all-start.2) | async-done | bytes 786464 | tf_op jit(solution)/shard_map/all_to_all | solution.py:58
  272.2 2.0 gather_fusion
  275.2 3.2 %convolution_convert_fusion.1 = bf16[128,2048]{1,0:T(8,128)(2,1)} fusion(bf16[512,2048]{0,1:T(8,128)(2,1)} %all-gather.2.cloned.1.call-done, bf16[128,512]{1,0:T(8,128)(2,1)S(1)} %multiply_reduce_fusion), kind=kOutput, calls=%fused_computation.5 | convolution fusion | flops 268697600 | bytes 2752512 | tf_op jit(solution)/shard_map/dot_general | solution.py:65
  (37 shorter events, 13.1 us)
Async XLA Ops:
  7.2 151.1 %copy-start = (bf16[1,512,1408]{2,1,0:T(8,128)(2,1)S(1)}, bf16[1,512,1408]{2,1,0:T(8,128)(2,1)}, u32[]{:S(2)}) copy-start(bf16[1,512,1408]{2,1,0:T(8,128)(2,1)} %param.15) | copy-start | bytes 4325380
  9.6 19.3 %copy-start.5 = (s32[128,4]{0,1:T(4,128)S(1)}, s32[128,4]{0,1:T(4,128)}, u32[]{:S(2)}) copy-start(s32[128,4]{0,1:T(4,128)} %param.11) | copy-start | bytes 6148
  9.6 70.0 %all-to-all-start = ((bf16[128,16,512]{2,1,0:T(8,128)(2,1)}), bf16[128,16,512]{2,1,0:T(8,128)(2,1)S(1)}, u32[]{:S(2)}, u32[]{:S(2)}) async-start(bf16[128,16,512]{2,1,0:T(8,128)(2,1)} %stack.2), calls=%async_computation | async-start | bytes 4194304 | tf_op jit(solution)/shard_map/all_to_all | solution.py:10
  28.2 114.7 %all-gather.2.cloned.1.call-start = ((), (), s32[]{:S(2)}) async-start(), calls=%async_computation.5 | async-start | bytes 2113536 | tf_op jit(solution)/shard_map/all_gather | solution.py:32
  79.6 5.5 %copy-start.1 = (bf16[128,16,512]{2,1,0:T(8,128)(2,1)}, bf16[128,16,512]{2,1,0:T(8,128)(2,1)S(1)}, u32[]{:S(2)}) copy-start(bf16[128,16,512]{2,1,0:T(8,128)(2,1)S(1)} %all-to-all-done) | copy-start | bytes 6291460
  82.9 11.3 %copy-start.6 = (f32[128,4]{0,1:T(4,128)S(1)}, f32[128,4]{0,1:T(4,128)}, u32[]{:S(2)}) copy-start(f32[128,4]{0,1:T(4,128)} %param.12) | copy-start | bytes 6148
  85.1 57.7 %copy-start.4 = (bf16[128,2048]{1,0:T(8,128)(2,1)S(1)}, bf16[128,2048]{1,0:T(8,128)(2,1)}, u32[]{:S(2)}) copy-start(bf16[128,2048]{1,0:T(8,128)(2,1)} %param.17) | copy-start | bytes 1572868
  85.1 62.5 %all-to-all-start.1 = ((bf16[128,1,6,512]{3,2,1,0:T(8,128)(2,1)}), bf16[128,1,6,512]{3,2,1,0:T(8,128)(2,1)S(1)}, u32[]{:S(2)}, u32[]{:S(2)}) async-start(bf16[128,1,6,512]{3,2,1,0:T(8,128)(2,1)} %bitcast.57), calls=%async_computation.1 | async-start | bytes 2097152 | tf_op jit(solution)/shard_map/all_to_all | solution.py:49
  142.8 2.1 copy-start.3
  147.6 41.5 %all-to-all-start.3 = ((bf16[128,1,6,512]{3,2,1,0:T(8,128)(2,1)}), bf16[128,1,6,512]{3,2,1,0:T(8,128)(2,1)S(1)}, u32[]{:S(2)}, u32[]{:S(2)}) async-start(bf16[128,1,6,512]{3,2,1,0:T(8,128)(2,1)} %bitcast.10), calls=%async_computation.3 | async-start | bytes 2097152 | tf_op jit(solution)/shard_map/all_to_all | solution.py:72
  196.1 37.4 %all-to-all-start.4 = ((bf16[128,1,6,512]{3,2,1,0:T(8,128)(2,1)}), bf16[128,1,6,512]{3,2,1,0:T(8,128)(2,1)S(1)}, u32[]{:S(2)}, u32[]{:S(2)}) async-start(bf16[128,1,6,512]{3,2,1,0:T(8,128)(2,1)} %copy.51), calls=%async_computation.4 | async-start | bytes 2097152 | tf_op jit(solution)/shard_map/all_to_all | solution.py:81
  233.5 1.0 copy-start.2
  234.5 37.4 %all-to-all-start.2 = ((bf16[128,1,6,512]{3,2,1,0:T(8,128)(2,1)}), bf16[128,1,6,512]{3,2,1,0:T(8,128)(2,1)S(1)}, u32[]{:S(2)}, u32[]{:S(2)}) async-start(bf16[128,1,6,512]{3,2,1,0:T(8,128)(2,1)} %copy.46), calls=%async_computation.2 | async-start | bytes 2097152 | tf_op jit(solution)/shard_map/all_to_all | solution.py:58
Sparse Core Ops, SparseCore 0:
  32.1 110.6 all-gather.1
